TPU v7x, 256 devices: a whole 4x4x8 slice. The times are simulated.
256 devices in a mesh: dp: 8 (over x, core), tile: 32 (over z, y).
Axes of the slice: x: 4, y: 4, z: 8, core: 2. Of those that a mesh axis runs over, the one named last changes fastest.
Arguments:
- acts: bfloat16 [3840, 12, 4096], P(('dp', 'tile')), may hold values from -40 to 40
- grads: bfloat16 [3840, 12, 4096], P(('dp', 'tile')), may hold values from -40 to 40
- lengths: int32 [3840], P(('dp', 'tile')), may hold values from 0 to 12, as said below
- assign: int32 [3840], P(('dp', 'tile')), may hold values from -1 to 95, as said below
Outputs:
- act_factor: float32 [4096, 4096], P('tile', 'dp')
- grad_factor: float32 [4096, 4096], P('tile', 'dp')
- block_norms: float32 [3072], P(('dp', 'tile'))
Inputs may be any that keep to these rules, and one draw needn't show every extreme that they name: `lengths`: 0 exactly for an empty slot; a live block holds 1 to 12 tokens, its first ones; in each index of tile exactly 96 of the 120 slots are live, and one device of it has all 15 slots live. `assign`: -1 exactly for empty slots; within one index of tile the live blocks take each value 0 to 95 once; value q names index of dp q // 12, and the blocks of one device name one index of dp at most 2 times.
All inputs are finite; a program needn't handle non-finite values.
Results may differ from a plain program's by a relative error of at most 0.0003.
Values may be sent and summed in bfloat16 or wider, within the bound.
No kernel may reach another device: no remote copies, remote signals or barrier semaphores. Data moves between devices by JAX's collectives and lax.ppermute only.
A program may use at most 128 MiB of HBM per device.

v0:
```python
import jax
import jax.numpy as jnp
from jax import lax
from jax.sharding import PartitionSpec as P

KEEP = 12


def score_blocks(data_acts, data_grads):
    block_len = data_acts.shape[1]
    feat_width = data_acts.shape[2]
    self_acts = jnp.einsum("btw,bsw->bts", data_acts, data_acts, preferred_element_type=jnp.float32)
    self_grads = jnp.einsum(
        "btw,bsw->bts", data_grads, data_grads, preferred_element_type=jnp.float32
    )
    return jnp.sum(self_acts * self_grads, axis=(1, 2)) * (
        1.0 / (feat_width * feat_width * block_len)
    )


def inner_rows(left_part, right_part):
    return lax.dot_general(
        left_part, right_part, (((0,), (0,)), ((), ())), preferred_element_type=jnp.float32
    )


def body(acts, grads, lengths, assign):
    n_dp = lax.axis_size("dp")
    n_tile = lax.axis_size("tile")
    slot_count, block_len, feat_width = acts.shape
    capacity = -(-slot_count // n_dp)
    positions = jnp.arange(block_len, dtype=jnp.int32)
    live_tokens = (positions[None, :] < lengths[:, None]).astype(jnp.bfloat16)[:, :, None]
    masked_acts = acts * live_tokens
    masked_grads = grads * live_tokens
    target_dp = jnp.where(assign >= 0, assign // KEEP, -1)
    target_slot = jnp.where(assign >= 0, assign % KEEP, -1)
    to_peer = target_dp[:, None] == jnp.arange(n_dp, dtype=jnp.int32)[None, :]
    earlier = jnp.cumsum(to_peer.astype(jnp.int32), axis=0) - 1
    peer_rank = jnp.sum(jnp.where(to_peer, earlier, 0), axis=1)
    routing = to_peer.T[:, None, :] & (
        peer_rank[None, None, :] == jnp.arange(capacity, dtype=jnp.int32)[None, :, None]
    )
    send_slot = jnp.sum(routing.astype(jnp.int32) * (target_slot[None, None, :] + 1), axis=2) - 1
    keep_ids = jnp.arange(KEEP, dtype=jnp.int32)[:, None]
    local_scores = score_blocks(masked_acts, masked_grads)
    send_score = jnp.sum(jnp.where(routing, local_scores[None, None, :], 0.0), axis=2)
    got_score, got_slot = (
        lax.all_to_all(send_score, "dp", split_axis=0, concat_axis=0, tiled=True),
        lax.all_to_all(send_slot, "dp", split_axis=0, concat_axis=0, tiled=True),
    )
    placing = got_slot.reshape(-1)[None, :] == keep_ids
    block_norms = jnp.sum(jnp.where(placing, got_score.reshape(-1)[None, :], 0.0), axis=1)
    flat_acts = masked_acts.reshape(-1, feat_width)
    flat_grads = masked_grads.reshape(-1, feat_width)
    col_span = feat_width // n_dp
    col_start = lax.axis_index("dp") * col_span
    group_acts, group_grads = (
        lax.all_gather(flat_acts, "dp", axis=0, tiled=True),
        lax.all_gather(flat_grads, "dp", axis=0, tiled=True),
    )
    cols_acts = lax.dynamic_slice_in_dim(group_acts, col_start, col_span, 1)
    cols_grads = lax.dynamic_slice_in_dim(group_grads, col_start, col_span, 1)
    summed = lax.psum_scatter(
        jnp.concatenate(
            [inner_rows(group_acts, cols_acts), inner_rows(group_grads, cols_grads)], axis=1
        ),
        "tile",
        scatter_dimension=0,
        tiled=True,
    )
    scale = 1.0 / (n_dp * n_tile * KEEP * block_len)
    act_factor = summed[:, :col_span] * scale
    grad_factor = summed[:, col_span:] * scale
    return (act_factor, grad_factor, block_norms)


def solution(mesh):
    in_specs = (
        P(("dp", "tile"), None, None),
        P(("dp", "tile"), None, None),
        P(("dp", "tile")),
        P(("dp", "tile")),
    )
    out_specs = (P("tile", "dp"), P("tile", "dp"), P(("dp", "tile")))
    return jax.shard_map(body, mesh=mesh, in_specs=in_specs, out_specs=out_specs, check_vma=False)
```

profile of v0, /device:TPU:6, one launch (start us, length us, event | category | flops | bytes accessed | tf_op | source)
XLA Modules:
  0.0 435.5 jit_solution(13397794448862124536)
XLA Ops:
  7.2 0.7 fusion.7
  7.9 3.3 broadcast_multiply_fusion.1
  11.2 0.9 copy.36
  12.1 1.4 reshape.102
  13.6 2.3 copy.35
  15.9 1.4 reshape.100
  17.4 65.1 %all-gather.7.cloned.1.call-done = bf16[8,180,4096]{2,1,0:T(8,128)(2,1)} async-done(((bf16[1,180,4096]{2,1,0:T(8,128)(2,1)}), bf16[8,180,4096]{2,1,0:T(8,128)(2,1)}) %all-gather.7.cloned.1.call-update) | async-done | bytes 11796496 | tf_op jit(solution)/shard_map/all_gather | solution.py:60
  82.5 9.7 %reshape.103 = bf16[1440,4096]{1,0:T(8,128)(2,1)} reshape(bf16[8,180,4096]{2,1,0:T(8,128)(2,1)} %all-gather.7.cloned.1.call-done) | data formatting | bytes 23592960
  92.2 12.0 %fusion = f32[4096,512]{0,1:T(8,128)} fusion(bf16[1440,4096]{1,0:T(8,128)(2,1)} %reshape.103, s32[]{:T(128)S(6)} %select_n.35), kind=kOutput, calls=%fused_computation.1 | convolution fusion | flops 6039797760 | bytes 21659652 | tf_op jit(solution)/shard_map/dot_general | solution.py:22
  104.2 48.2 %all-gather.5.cloned.1.call-done = bf16[8,180,4096]{2,1,0:T(8,128)(2,1)} async-done(((bf16[1,180,4096]{2,1,0:T(8,128)(2,1)}), bf16[8,180,4096]{2,1,0:T(8,128)(2,1)}) %all-gather.5.cloned.1.call-update) | async-done | bytes 11796496 | tf_op jit(solution)/shard_map/all_gather | solution.py:59
  152.4 9.6 %reshape.101 = bf16[1440,4096]{1,0:T(8,128)(2,1)} reshape(bf16[8,180,4096]{2,1,0:T(8,128)(2,1)} %all-gather.5.cloned.1.call-done) | data formatting | bytes 23592960
  162.0 10.7 %fusion.2 = f32[4096,512]{0,1:T(8,128)S(1)} fusion(bf16[1440,4096]{1,0:T(8,128)(2,1)} %reshape.101, s32[]{:T(128)S(6)} %select_n.35), kind=kOutput, calls=%fused_computation.3 | convolution fusion | flops 6039797760 | bytes 21659652 | tf_op jit(solution)/shard_map/dot_general | solution.py:22
  172.7 6.3 %pad_maximum_fusion = f32[4096,1024]{0,1:T(8,128)} fusion(f32[4096,512]{0,1:T(8,128)S(1)} %copy-done, f32[4096,512]{0,1:T(8,128)S(1)} %fusion.2), kind=kLoop, calls=%fused_computation | loop fusion | flops 4194304 | bytes 33554432 | tf_op jit(solution)/shard_map/concatenate | solution.py:65
  180.0 0.7 copy.37
  180.7 5.7 %all-to-all-start = ((s32[8,1,2]{2,1,0:T(1,128)}), s32[8,1,2]{2,1,0:T(1,128)S(1)}, u32[]{:S(2)}, u32[]{:S(2)}) async-start(s32[8,1,2]{2,1,0:T(1,128)} %copy.37), calls=%async_computation.1 | async-start | bytes 8192 | tf_op jit(solution)/shard_map/all_to_all | solution.py:50
  186.4 1.6 fusion.13
  188.0 1.8 fusion.4
  189.9 0.7 copy.42
  190.6 4.8 %all-to-all-start.1 = ((f32[8,1,2]{2,1,0:T(1,128)}), f32[8,1,2]{2,1,0:T(1,128)S(1)}, u32[]{:S(2)}, u32[]{:S(2)}) async-start(f32[8,1,2]{2,1,0:T(1,128)} %copy.42), calls=%async_computation.2 | async-start | bytes 8192 | tf_op jit(solution)/shard_map/all_to_all | solution.py:49
  196.7 1.9 all-to-all-done.1
  200.4 225.8 %reduce-scatter.2.cloned.1.call-done = f32[128,1024]{0,1:T(8,128)} async-done(((f32[4096,1024]{0,1:T(8,128)}), f32[128,1024]{0,1:T(8,128)}) %reduce-scatter.2.cloned.1.call-update) | async-done | bytes 524304 | tf_op jit(solution)/shard_map/reduce_scatter | solution.py:64
  426.2 1.1 slice_multiply_fusion
  427.3 0.8 copy.44
  428.2 0.8 copy.43
  (30 shorter events, 4.4 us)
Async XLA Ops:
  7.2 75.3 %all-gather.7.cloned.1.call-start = ((), (), s32[]{:S(2)}) async-start(), calls=%async_computation.5 | async-start | bytes 13565952 | tf_op jit(solution)/shard_map/all_gather | solution.py:60
  13.5 138.9 %all-gather.5.cloned.1.call-start = ((), (), s32[]{:S(2)}) async-start(), calls=%async_computation.4 | async-start | bytes 13565952 | tf_op jit(solution)/shard_map/all_gather | solution.py:59
  17.4 408.9 %reduce-scatter.2.cloned.1.call-start = ((), (), s32[]{:S(2)}) async-start(), calls=%async_computation.3 | async-start | bytes 17301504 | tf_op jit(solution)/shard_map/reduce_scatter | solution.py:64
  162.0 10.7 %copy-start = (f32[4096,512]{0,1:T(8,128)S(1)}, f32[4096,512]{0,1:T(8,128)}, u32[]{:S(2)}) copy-start(f32[4096,512]{0,1:T(8,128)} %fusion) | copy-start | bytes 25165828
  179.0 0.7 copy-start.2
  179.0 7.4 %copy-start.1 = (bf16[15,12,4096]{2,0,1:T(8,128)(2,1)S(1)}, bf16[15,12,4096]{2,0,1:T(8,128)(2,1)}, u32[]{:S(2)}) copy-start(bf16[15,12,4096]{2,0,1:T(8,128)(2,1)} %get-tuple-element.17) | copy-start | bytes 4423684
  180.7 9.9 %all-to-all-start = ((s32[8,1,2]{2,1,0:T(1,128)}), s32[8,1,2]{2,1,0:T(1,128)S(1)}, u32[]{:S(2)}, u32[]{:S(2)}) async-start(s32[8,1,2]{2,1,0:T(1,128)} %copy.37), calls=%async_computation.1 | async-start | bytes 8192 | tf_op jit(solution)/shard_map/all_to_all | solution.py:50
  190.6 7.9 %all-to-all-start.1 = ((f32[8,1,2]{2,1,0:T(1,128)}), f32[8,1,2]{2,1,0:T(1,128)S(1)}, u32[]{:S(2)}, u32[]{:S(2)}) async-start(f32[8,1,2]{2,1,0:T(1,128)} %copy.42), calls=%async_computation.2 | async-start | bytes 8192 | tf_op jit(solution)/shard_map/all_to_all | solution.py:49
Sparse Core Ops, SparseCore 0:
  13.7 68.7 all-gather.6
  84.3 68.0 all-gather.4
  179.1 247.0 reduce-scatter.1
where the time goes:
time: 436 us
  waiting for transfers between devices  341 us (78%)
  local copies, waits for them, and re-layouts  30.1 us (7%)
  matrix products  26.1 us (6%)
  other arithmetic  13.8 us (3%)
  between operations  13.8 us (3%)
  starting transfers between devices  10.6 us (2%)
    reduce_scatter x1, waiting for transfers between devices, body(): lax.psum_scatter(jnp.concatenate([inner_rows(group_acts, cols_acts), inne...  226 us
    all_gather x1, waiting for transfers between devices, body(): lax.all_gather(flat_grads, 'dp', axis=0, tiled=True)  65.1 us
    all_gather x1, waiting for transfers between devices, body(): lax.all_gather(flat_acts, 'dp', axis=0, tiled=True)  48.2 us
    unnamed x12, local copies, waits for them, and re-layouts  24.4 us
    dot_general x2, matrix products, inner_rows(): lax.dot_general(left_part, right_part, (((0,), (0,)), ((), ())), preferre...  22.7 us
  transfers between devices with their start and end apart: 5, of which 4 were waited for; matrix products, arithmetic and copies ran while one was open for 8% of the time, Pallas kernels for 0%

commit v1 on v0

v1 whole, which is shorter than its diff:
```python
import functools

import jax
import jax.numpy as jnp
from jax import lax
from jax.experimental import pallas as pl
from jax.experimental.pallas import tpu as pltpu
from jax.sharding import PartitionSpec as P

KEEP = 12
NX, NK, NZ, NY = 4, 2, 8, 4
AXES = ("dp", "tile")
VMEM_BYTES = 26 * 1024 * 1024


def route(x=0, k=0, z=0, y=0, fan=None):
    pairs = []
    for sx in range(NX):
        for sk in range(NK):
            for sz in range(NZ):
                for sy in range(NY):
                    step = 1 - 2 * sk
                    tx = (sx + x + step * (fan == "x")) % NX
                    ty = (sy + y + step * (fan == "y")) % NY
                    tk, tz = (sk + k) % NK, (sz + z) % NZ
                    source = ((sx * NK + sk) * NZ + sz) * NY + sy
                    pairs.append((source, ((tx * NK + tk) * NZ + tz) * NY + ty))
    return pairs


def send(value, **shift):
    return lax.ppermute(value, AXES, route(**shift))


def token_rows(tokens, live):
    slots, count, width = tokens.shape
    by_position = jnp.pad(jnp.transpose(tokens, (1, 0, 2)), ((0, 0), (0, 16 - slots), (0, 0)))
    return jnp.where(live, by_position, 0).reshape(count * 16, width)


def block_scores(rows_a, rows_g, count):
    def gram(rows):
        return lax.dot_general(
            rows, rows, (((1,), (1,)), ((), ())), preferred_element_type=jnp.float32
        )

    slot = jnp.arange(rows_a.shape[0], dtype=jnp.int32) % 16
    same = slot[:, None] == slot[None, :]
    per_row = jnp.sum(jnp.where(same, gram(rows_a) * gram(rows_g), 0.0), axis=1)
    width = rows_a.shape[1]
    return jnp.sum(per_row.reshape(count, 16), axis=0) * (1.0 / (width * width * count))


def load(pieces, buf, sems):
    copies, start = [], 0
    for i, piece in enumerate(pieces):
        copies.append(pltpu.make_async_copy(piece, buf.at[pl.ds(start, piece.shape[0])], sems.at[i]))
        start += piece.shape[0]
    for copy in copies:
        copy.start()
    for copy in copies:
        copy.wait()


def largest(buf):
    def step(i, so_far):
        return jnp.maximum(so_far, jnp.abs(buf[pl.ds(pl.multiple_of(i * 16, 16), 16), :]))

    zeros = jnp.zeros((16, buf.shape[1]), buf.dtype)
    return jnp.max(lax.fori_loop(0, buf.shape[0] // 16, step, zeros).astype(jnp.float32))


def lanes(place):
    return pl.ds(pl.multiple_of(place * 128, 128), 128)


def load_and_turn(acts, at, pieces, buf, left, picked, sems):
    load(pieces, buf, sems)
    if acts:
        left[...] = jnp.transpose(buf[:, pl.ds(pl.multiple_of(at[0] * 1024, 1024), 1024)])
        for role in range(4):
            for i in range(4):
                unit = (role * 4 + i) * 128
                picked[:, unit : unit + 128] = buf[:, lanes(unit_tile(role, i, at))]
    else:
        for z in range(NZ):
            left[z * 128 : (z + 1) * 128, :] = jnp.transpose(buf[:, lanes(lax.rem(z + at[2], NZ) * 4 + at[0])])


def target_of(role, at):
    ahead = jnp.where(at[3] == 0, 1, 3)
    away = jnp.where(role == 0, 2, jnp.where(role == 3, 0, ahead))
    return lax.rem(at[1] + away, 4)


def half_of(role, at):
    return jnp.where(role == 1, 1 - at[3], at[3])


def unit_tile(role, i, at):
    z = lax.rem(half_of(role, at) * 4 + i + at[2], NZ)
    return z * 4 + target_of(role, at)


def products(acts, at, buf, left, picked, store):
    role = pl.program_id(0)
    if acts:
        columns = picked[:, pl.ds(pl.multiple_of(role * 512, 512), 512)]
        out = jnp.dot(left[...], columns, preferred_element_type=jnp.float32)
        for i in range(4):
            store(i, slice(0, 1024), out[:, i * 128 : (i + 1) * 128])
        return
    rows = left[pl.ds(pl.multiple_of(half_of(role, at) * 512, 512), 512), :]
    for core in range(2):
        start = pl.multiple_of((2 * target_of(role, at) + core) * 512, 512)
        out = jnp.dot(rows, buf[:, pl.ds(start, 512)], preferred_element_type=jnp.float32)
        for i in range(4):
            for part in range(4):
                tile = out[i * 128 : (i + 1) * 128, part * 128 : (part + 1) * 128]
                store(i, slice((core * 4 + part) * 128, (core * 4 + part + 1) * 128), tile)


def early_kernel(at, *refs, count, acts):
    pieces, (out, peak, buf, left, picked, sems) = refs[:count], refs[count:]

    @pl.when(pl.program_id(0) == 0)
    def _():
        load_and_turn(acts, at, pieces, buf, left, picked, sems)
        peak[...] = jnp.full(peak.shape, largest(buf), jnp.float32)

    def store(i, rows, value):
        out[0, i, rows] = value

    products(acts, at, buf, left, picked, store)


def late_kernel(at, early_peak, early, *refs, count, acts, tokens):
    pieces, (sent, kept, buf, left, picked, exponent, sems) = refs[:count], refs[count:]

    @pl.when(pl.program_id(0) == 0)
    def _():
        load_and_turn(acts, at, pieces, buf, left, picked, sems)
        peak = jnp.maximum(early_peak[0:1, :], largest(buf))
        bound = tokens * jnp.maximum(peak * peak, 1e-35)
        exponent[...] = jnp.broadcast_to(jnp.floor(jnp.log2(30000.0 / bound)), exponent.shape)

    def into(out, scale):
        def store(i, rows, value):
            out[0, i, rows] = (early[0, i, rows] + value) * scale

        products(acts, at, buf, left, picked, store)
        for i in range(4):
            out[0, i, 1024:1040] = exponent[...]

    @pl.when(pl.program_id(0) < 2)
    def _():
        into(sent, jnp.exp2(exponent[0:1, :]))

    @pl.when(pl.program_id(0) >= 2)
    def _():
        into(kept, 1.0)


def product(acts, at, pieces, early=(), tokens=None):
    count, rows, width = len(pieces), sum(p.shape[0] for p in pieces), pieces[0].shape[1]
    peak_spec = pl.BlockSpec((8, 128), lambda i, at: (0, 0))
    peak_shape = jax.ShapeDtypeStruct((8, 128), jnp.float32)
    spec = pl.BlockSpec((1, 4, 1024, 128), lambda i, at: (i, 0, 0, 0))
    scratch = [
        pltpu.VMEM((rows, width), jnp.bfloat16),
        pltpu.VMEM((1024, rows), jnp.bfloat16),
        pltpu.VMEM((rows, 2048) if acts else (16, 128), jnp.bfloat16),
    ]
    if early:
        kernel = functools.partial(late_kernel, tokens=tokens)
        before = [peak_spec, spec]
        out_specs = [
            pl.BlockSpec((1, 4, 1040, 128), lambda i, at: (jnp.minimum(i, 1), 0, 0, 0)),
            pl.BlockSpec((1, 4, 1040, 128), lambda i, at: (jnp.maximum(i - 2, 0), 0, 0, 0)),
        ]
        out_shape = [jax.ShapeDtypeStruct((2, 4, 1040, 128), jnp.float32)] * 2
        scratch.append(pltpu.VMEM((16, 128), jnp.float32))
        cost = pl.CostEstimate(
            flops=2 * rows * 1024 * 2048, bytes_accessed=2 * rows * width + 2 * 2048 * 4096, transcendentals=0
        )
    else:
        kernel, before = early_kernel, []
        out_specs = [spec, peak_spec]
        out_shape = [jax.ShapeDtypeStruct((4, 4, 1024, 128), jnp.float32), peak_shape]
        cost = pl.CostEstimate(flops=1, bytes_accessed=1, transcendentals=0)
    return pl.pallas_call(
        functools.partial(kernel, count=count, acts=acts),
        grid_spec=pltpu.PrefetchScalarGridSpec(
            num_scalar_prefetch=1,
            grid=(4,),
            in_specs=before + [pl.BlockSpec(memory_space=pltpu.HBM)] * count,
            out_specs=out_specs,
            scratch_shapes=scratch + [pltpu.SemaphoreType.DMA((count,))],
        ),
        out_shape=out_shape,
        compiler_params=pltpu.CompilerParams(vmem_limit_bytes=VMEM_BYTES),
        cost_estimate=cost,
    )(at, *early, *[pltpu.with_memory_space_constraint(p, pltpu.HBM) for p in pieces])


def gather_line(rows, axis):
    other = send(rows, k=1)
    first = send(rows, fan=axis)
    second = send(other, fan=axis)
    far = send(first, fan=axis)
    return [rows, other, first, send(first, k=1)], [second, far]


def both_cores(pieces):
    return pieces + [send(piece, k=1) for piece in pieces]


def reduce_line(sent, kept, axis, core):
    half, span = NZ // 2, 512

    def exponent(rows):
        return rows[:, -1:].astype(jnp.float32)

    def opened(rows):
        return rows[:, :-16].astype(jnp.float32) * jnp.exp2(-exponent(rows))

    def columns(value, core):
        return lax.dynamic_slice_in_dim(value, core * span, span, 1)

    received = send(sent, fan=axis)
    relay, plain = received[:half], received[half:]
    both = jnp.minimum(exponent(kept[0]), exponent(relay)) - 1.0
    is_exponent = jnp.arange(1040, dtype=jnp.int32)[None, :, None] >= 1024
    total = kept[0] + relay.astype(jnp.float32) * jnp.exp2(-exponent(relay))
    last = send(jnp.where(is_exponent, both, total * jnp.exp2(both)).astype(jnp.float16), fan=axis)
    plain = opened(plain)
    other_own, other_plain = send(
        jnp.stack([columns(kept[1], 1 - core), columns(plain, 1 - core)]), k=1
    )
    other_last = send(jnp.concatenate([columns(last, 1 - core), last[:, -16:]], axis=1), k=1)
    this_half = columns(kept[1], core) + other_plain + columns(opened(last), core)
    other_half = columns(plain, core) + other_own + opened(other_last)
    return jnp.concatenate(
        [jnp.where(core == 0, this_half, other_half), jnp.where(core == 0, other_half, this_half)], axis=0
    )


def reduce_z(value, beside):
    up, down = send(value[4, :1], z=1), send(value[4, 1:], z=-1)
    up = send(jnp.concatenate([value[3, :1] + up, value[3, 1:]], axis=0), z=1)
    down = send(jnp.concatenate([value[5, :1], value[5, 1:] + down], axis=0), z=-1)
    up, down, beside = lax.optimization_barrier((up, down, beside))
    up, down = send(value[2] + up, z=1), send(value[6] + down, z=-1)
    up, down = send(value[1] + up, z=1), send(value[7] + down, z=-1)
    return value[0] + up + down, beside


def body(acts, grads, lengths, assign):
    n_dp = lax.axis_size("dp")
    n_tile = lax.axis_size("tile")
    slot_count, block_len, feat_width = acts.shape
    dp, tile = lax.axis_index("dp"), lax.axis_index("tile")
    my_x, my_k = dp // NK, dp % NK
    my_z, my_y = tile // NY, tile % NY
    positions = jnp.arange(block_len, dtype=jnp.int32)
    live = (positions[:, None] < jnp.pad(lengths, (0, 16 - slot_count))[None, :])[:, :, None]
    rows_a, rows_g = token_rows(acts, live), token_rows(grads, live)
    early_a, late_a = gather_line(rows_a, "x")
    early_g, late_g = gather_line(rows_g, "y")

    scores = block_scores(rows_a, rows_g, block_len)[:slot_count]
    places = jnp.arange(n_dp * KEEP, dtype=jnp.int32)
    placed = jnp.sum(jnp.where(assign[:, None] == places[None, :], scores[:, None], 0.0), axis=0)
    got = lax.all_to_all(placed.reshape(n_dp, KEEP), "dp", split_axis=0, concat_axis=0, tiled=True)
    block_norms = jnp.sum(got, axis=0)

    at_a = jnp.stack([my_x, my_y, my_z, my_k])
    at_g = jnp.stack([my_y, my_x, my_z, my_k])
    sum_a, sum_g = product(True, at_a, early_a), product(False, at_g, early_g)
    late_a, late_g, sum_a, sum_g = lax.optimization_barrier((late_a, late_g, sum_a, sum_g))
    tokens = n_dp * slot_count * block_len
    sent_a, kept_a = product(True, at_a, both_cores(late_a), sum_a[::-1], tokens)
    sent_a = sent_a.astype(jnp.float16).reshape(NZ, 1040, 128)
    sent_a, kept_a, late_g, sum_g = lax.optimization_barrier((sent_a, kept_a, both_cores(late_g), sum_g))
    sent_g, kept_g = product(False, at_g, late_g, sum_g[::-1], tokens)
    sent_g = sent_g.astype(jnp.float16).reshape(NZ, 1040, 128)
    factor = 1.0 / (n_dp * n_tile * KEEP * block_len)
    line_a = reduce_line(sent_a, kept_a, "y", my_k) * factor
    line_g = reduce_line(sent_g, kept_g, "x", my_k) * factor
    total, block_norms = reduce_z(jnp.stack([line_a, line_g], axis=1), block_norms)
    act_factor = jnp.transpose(total[0])
    grad_factor = jnp.concatenate([total[1, at : at + 128] for at in range(0, 512, 128)], axis=1)
    return (act_factor, grad_factor, block_norms)


def solution(mesh):
    in_specs = (
        P(("dp", "tile"), None, None),
        P(("dp", "tile"), None, None),
        P(("dp", "tile")),
        P(("dp", "tile")),
    )
    out_specs = (P("tile", "dp"), P("tile", "dp"), P(("dp", "tile")))
    return jax.shard_map(body, mesh=mesh, in_specs=in_specs, out_specs=out_specs, check_vma=False)
```

time: 436 us -> 217 us (0.50)
  waiting for transfers between devices: 341 us -> 100 us
  Pallas kernels: 0 us -> 37.8 us
  matrix products: 26.1 us -> 1.19 us
  starting transfers between devices: 10.6 us -> 29.4 us
  local copies, waits for them, and re-layouts: 30.1 us -> 14.1 us
  between operations: 13.8 us -> 1.2 us
  other arithmetic: 13.8 us -> 22.3 us
  blocking collectives: 0 us -> 8.32 us
    reduce_scatter x1 -> x0, waiting for transfers between devices: 226 us -> none  [body(): lax.psum_scatter(jnp.concatenate([inner_rows(group_acts, cols_acts), inne...]
    all_gather x2 -> x0, waiting for transfers between devices: 113 us -> none  [the longest x1 65.1 us: body(): lax.all_gather(flat_grads, 'dp', axis=0, tiled=True)]
    ppermute x0 -> x30, waiting for transfers between devices: none -> 100 us  [send(): return lax.ppermute(value, AXES, route(**shift))]
    pallas_call x0 -> x4, Pallas kernels: none -> 37.8 us  [product(): pl.pallas_call(functools.partial(kernel, count=count, acts=acts), grid_sp...]
    ppermute x0 -> x30, starting transfers between devices: none -> 29.4 us  [send(): return lax.ppermute(value, AXES, route(**shift))]
    dot_general x4 -> x2, matrix products: 26.1 us -> 1.19 us  [gram(): lax.dot_general(rows, rows, (((1,), (1,)), ((), ())), preferred_element_t...]
    unnamed x12 -> x43, local copies, waits for them, and re-layouts: 24.4 us -> 8.07 us
    all_to_all x2 -> x0, starting transfers between devices: 10.5 us -> none  [the longest x1 5.66 us: body(): lax.all_to_all(send_slot, 'dp', split_axis=0, concat_axis=0, tiled=True)]
  transfers between devices with their start and end apart: 5 -> 30, of which waited for: 4 -> 17; matrix products, arithmetic and copies ran while one was open for 8% -> 9% of each run, Pallas kernels for 0% -> 18%
where the time goes in v1:
time: 217 us; the launch traced here: 214 us
  waiting for transfers between devices  100 us (46%)
  Pallas kernels  37.8 us (17%)
  starting transfers between devices  29.4 us (14%)
  other arithmetic  22.3 us (10%)
  local copies, waits for them, and re-layouts  14.1 us (6%)
  blocking collectives  8.32 us (4%)
    ppermute x30, waiting for transfers between devices, send(): return lax.ppermute(value, AXES, route(**shift))  100 us
    pallas_call x4, Pallas kernels, product(): pl.pallas_call(functools.partial(kernel, count=count, acts=acts), grid_sp...  37.8 us
    ppermute x30, starting transfers between devices, send(): return lax.ppermute(value, AXES, route(**shift))  29.4 us
    all_to_all x1, blocking collectives, body(): lax.all_to_all(placed.reshape(n_dp, KEEP), 'dp', split_axis=0, concat_axi...  8.32 us
    unnamed x43, local copies, waits for them, and re-layouts  8.07 us
  transfers between devices with their start and end apart: 30, of which 17 were waited for; matrix products, arithmetic and copies ran while one was open for 9% of the time, Pallas kernels for 18%

profile of v1, /device:TPU:6, one launch (start us, length us, event | category | flops | bytes accessed | tf_op | source)
XLA Modules:
  0.0 214.4 jit_solution(4958001499784024916)
XLA Ops:
  1.3 2.7 %pad_select_fusion = (bf16[12,16,4096]{2,1,0:T(8,128)(2,1)S(1)}, bf16[12,16,4096]{2,1,0:T(8,128)(2,1)S(1)}) fusion(bf16[12,15,4096]{2,1,0:T(8,128)(2,1)} %bitcast.130, pred[12,16]{1,0:T(8,128)(4,1)S(1)} %iota_compare_fusion.2, bf16[12,15,4096]{2,1,0:T(8,128)(2,1)} %bitcast.131), kind=kLoop, calls=%fused_computation.12 | loop fusion | flops 1572864 | bytes 6095040 | tf_op jit(solution)/shard_map/jit(_where)/select_n | solution.py:38
  7.2 18.6 %collective-permute-done.6.refs_2_ = bf16[192,4096]{1,0:T(8,128)(2,1)} collective-permute-done((bf16[192,4096]{1,0:T(8,128)(2,1)S(1)}, bf16[192,4096]{1,0:T(8,128)(2,1)}, u32[]{:S(2)}, u32[]{:S(2)}) %collective-permute-start.6) | collective-permute-done | bytes 1572896 | tf_op jit(solution)/shard_map/ppermute | solution.py:32
  31.2 9.0 %shard_map.68 = (f32[4,4,1024,128]{3,2,1,0:T(8,128)S(1)}, f32[8,128]{1,0:T(8,128)S(1)}) custom-call(s32[4]{0:T(128)S(1)} %add_add_fusion.1.at, bf16[192,4096]{1,0:T(8,128)(2,1)} %bitcast.128, bf16[192,4096]{1,0:T(8,128)(2,1)} %collective-permute-done.4.refs_1_, bf16[192,4096]{1,0:T(8,128)(2,1)} %collective-permute-done.6.refs_2_, ...), custom_call_target="tpu_custom_call" | custom-call | flops 1 | bytes 1 | tf_op jit(solution)/shard_map/pallas_call | solution.py:191
  40.3 9.7 %shard_map.67 = (f32[4,4,1024,128]{3,2,1,0:T(8,128)S(1)}, f32[8,128]{1,0:T(8,128)S(1)}) custom-call(s32[4]{0:T(128)S(1)} %add_add_fusion.at, bf16[192,4096]{1,0:T(8,128)(2,1)} %bitcast.120, bf16[192,4096]{1,0:T(8,128)(2,1)} %collective-permute-done.refs_1_, bf16[192,4096]{1,0:T(8,128)(2,1)} %collective-permute-done.2.refs_2_, ...), custom_call_target="tpu_custom_call" | custom-call | flops 1 | bytes 1 | tf_op jit(solution)/shard_map/pallas_call | solution.py:191
  50.0 14.9 %collective-permute-done.1.refs_0_ = bf16[192,4096]{1,0:T(8,128)(2,1)} collective-permute-done((bf16[192,4096]{1,0:T(8,128)(2,1)}, bf16[192,4096]{1,0:T(8,128)(2,1)}, u32[]{:S(2)}, u32[]{:S(2)}) %collective-permute-start.1) | collective-permute-done | bytes 1572896 | tf_op jit(solution)/shard_map/ppermute | solution.py:32
  64.9 2.5 %collective-permute-done.5.refs_0_ = bf16[192,4096]{1,0:T(8,128)(2,1)} collective-permute-done((bf16[192,4096]{1,0:T(8,128)(2,1)}, bf16[192,4096]{1,0:T(8,128)(2,1)}, u32[]{:S(2)}, u32[]{:S(2)}) %collective-permute-start.5) | collective-permute-done | bytes 1572896 | tf_op jit(solution)/shard_map/ppermute | solution.py:32
  68.4 2.6 %collective-permute-done.10.refs_2_ = bf16[192,4096]{1,0:T(8,128)(2,1)S(1)} collective-permute-done((bf16[192,4096]{1,0:T(8,128)(2,1)}, bf16[192,4096]{1,0:T(8,128)(2,1)S(1)}, u32[]{:S(2)}, u32[]{:S(2)}) %collective-permute-start.10) | collective-permute-done | bytes 1572896 | tf_op jit(solution)/shard_map/ppermute | solution.py:32
  71.0 2.2 %collective-permute-done.11.refs_3_ = bf16[192,4096]{1,0:T(8,128)(2,1)S(1)} collective-permute-done((bf16[192,4096]{1,0:T(8,128)(2,1)}, bf16[192,4096]{1,0:T(8,128)(2,1)S(1)}, u32[]{:S(2)}, u32[]{:S(2)}) %collective-permute-start.11) | collective-permute-done | bytes 1572896 | tf_op jit(solution)/shard_map/ppermute | solution.py:32
  74.4 9.9 %shard_map.69 = (f32[2,4,1040,128]{3,2,1,0:T(8,128)S(1)}, f32[2,4,1040,128]{3,2,1,0:T(8,128)S(1)}) custom-call(s32[4]{0:T(128)S(1)} %add_add_fusion.at, f32[8,128]{1,0:T(8,128)S(1)} %get-tuple-element.34.early_peak, f32[4,4,1024,128]{3,2,1,0:T(8,128)S(1)} %get-tuple-element.35.early, bf16[192,4096]{1,0:T(8,128)(2,1)} %collective-permute-done.1.refs_0_, ...), custom_call_target="tpu_custom_call" | custom-call | flops 3221225472 | bytes 23068672 | tf_op jit(solution)/shard_map/pallas_call | solution.py:191
  88.6 9.2 %shard_map.70 = (f32[2,4,1040,128]{3,2,1,0:T(8,128)S(1)}, f32[2,4,1040,128]{3,2,1,0:T(8,128)S(1)}) custom-call(s32[4]{0:T(128)S(1)} %add_add_fusion.1.at, f32[8,128]{1,0:T(8,128)S(1)} %get-tuple-element.46.early_peak, f32[4,4,1024,128]{3,2,1,0:T(8,128)S(1)} %get-tuple-element.47.early, bf16[192,4096]{1,0:T(8,128)(2,1)} %collective-permute-done.5.refs_0_, ...), custom_call_target="tpu_custom_call" | custom-call | flops 3221225472 | bytes 23068672 | tf_op jit(solution)/shard_map/pallas_call | solution.py:191
  101.1 2.8 %fusion.39 = (f32[1,4,1040,128]{3,2,1,0:T(8,128)S(1)}, f32[4,1040,128]{2,1,0:T(8,128)S(1)}) fusion(f32[2,4,1040,128]{3,2,1,0:T(8,128)} %copy-done), kind=kLoop, calls=%fused_computation.105 | loop fusion | bytes 8519680 | tf_op jit(solution)/shard_map/slice | solution.py:241
  104.4 10.6 %collective-permute-done.14 = f16[8,1040,128]{2,1,0:T(8,128)(2,1)} collective-permute-done((f16[8,1040,128]{2,1,0:T(8,128)(2,1)}, f16[8,1040,128]{2,1,0:T(8,128)(2,1)}, u32[]{:S(2)}, u32[]{:S(2)}) %collective-permute-start.14) | collective-permute-done | bytes 2129952 | tf_op jit(solution)/shard_map/ppermute | solution.py:32
  115.8 11.4 %collective-permute-done.18 = f16[8,1040,128]{2,1,0:T(8,128)(2,1)} collective-permute-done((f16[8,1040,128]{2,1,0:T(8,128)(2,1)}, f16[8,1040,128]{2,1,0:T(8,128)(2,1)}, u32[]{:S(2)}, u32[]{:S(2)}) %collective-permute-start.18) | collective-permute-done | bytes 2129952 | tf_op jit(solution)/shard_map/ppermute | solution.py:32
  128.0 2.7 %select_convert_fusion.1 = (f16[4,1040,128]{2,1,0:T(8,128)(2,1)S(1)}, f16[4,1040,128]{2,1,0:T(8,128)(2,1)S(1)}) fusion(f16[8,1040,128]{2,1,0:T(8,128)(2,1)} %collective-permute-done.14, f32[4,128]{1,0:T(4,128)S(1)} %bitcast.134, f32[4,128]{1,0:T(4,128)S(1)} %bitcast.133, f32[4,128]{1,0:T(4,128)S(1)} %bitcast.135, pred[1040]{0:T(1024)(128)(4,1)S(1)} %iota_compare_fusion.1, ...), kind=kLoop, calls=%fused_computation.2 | loop fusion | flops 6389760 | bytes 8533008 | tf_op jit(solution)/shard_map/convert_element_type | solution.py:235
  130.8 2.1 collective-permute-start.20
  137.1 9.9 %collective-permute-done.16 = f16[4,1040,128]{2,1,0:T(8,128)(2,1)S(1)} collective-permute-done((f16[4,1040,128]{2,1,0:T(8,128)(2,1)S(1)}, f16[4,1040,128]{2,1,0:T(8,128)(2,1)S(1)}, u32[]{:S(2)}, u32[]{:S(2)}) %collective-permute-start.16) | collective-permute-done | bytes 1064992 | tf_op jit(solution)/shard_map/ppermute | solution.py:32
  155.5 4.4 %collective-permute-start.24 = (f32[1,512,128]{2,1,0:T(8,128)}, f32[1,512,128]{2,1,0:T(8,128)}, u32[]{:S(2)}, u32[]{:S(2)}) collective-permute-start(f32[1,512,128]{2,1,0:T(8,128)} %slice.209), channel_id=1, source_target_pairs={{0,28},{1,29},{2,30},{3,31},{4,0},{5,1},{6,2},{7,3},{8,4},{9,5},{1... | collective-permute-start | bytes 786440 | tf_op jit(solution)/shard_map/ppermute | solution.py:32
  160.7 2.9 %collective-permute-done.22 = f32[1,512,128]{2,1,0:T(8,128)} collective-permute-done((f32[1,512,128]{2,1,0:T(8,128)}, f32[1,512,128]{2,1,0:T(8,128)}, u32[]{:S(2)}, u32[]{:S(2)}) %collective-permute-start.22) | collective-permute-done | bytes 262176 | tf_op jit(solution)/shard_map/ppermute | solution.py:32
  169.0 3.7 %collective-permute-start.25 = (f32[2,512,128]{2,1,0:T(8,128)}, f32[2,512,128]{2,1,0:T(8,128)}, u32[]{:S(2)}, u32[]{:S(2)}) collective-permute-start(f32[2,512,128]{2,1,0:T(8,128)} %pad_maximum_fusion.6), channel_id=1, source_target_pairs={{0,28},{1,29},{2,30},{3,31},{4,0},{5,1},{6,2},{7,3},{8,4},{9,5},{1... | collective-permute-start | bytes 1572872 | tf_op jit(solution)/shard_map/ppermute | solution.py:32
  172.9 8.3 %all_to_all.9 = f32[8,1,12]{2,1,0:T(1,128)S(1)} all-to-all(f32[8,1,12]{2,1,0:T(1,128)S(1)} %bitcast.132), channel_id=1, replica_groups=mesh['dp'=8,'tile'=32] {'dp'}, dimensions={0} | all-to-all | bytes 768 | tf_op jit(solution)/shard_map/all_to_all | solution.py:274
  185.0 2.5 %collective-permute-start.26 = (f32[2,512,128]{2,1,0:T(8,128)S(1)}, f32[2,512,128]{2,1,0:T(8,128)S(1)}, u32[]{:S(2)}, u32[]{:S(2)}) collective-permute-start(f32[2,512,128]{2,1,0:T(8,128)S(1)} %get-tuple-element.80), channel_id=1, source_target_pairs={{0,4},{1,5},{2,6},{3,7},{4,8},{5,9},{6,10},{7,11},{8,12},{9,13},{1... | collective-permute-start | bytes 1572872 | tf_op jit(solution)/shard_map/ppermute | solution.py:32
  188.9 10.6 %collective-permute-done.26 = f32[2,512,128]{2,1,0:T(8,128)S(1)} collective-permute-done((f32[2,512,128]{2,1,0:T(8,128)S(1)}, f32[2,512,128]{2,1,0:T(8,128)S(1)}, u32[]{:S(2)}, u32[]{:S(2)}) %collective-permute-start.26) | collective-permute-done | bytes 524320 | tf_op jit(solution)/shard_map/ppermute | solution.py:32
  200.8 2.1 collective-permute-start.29
  202.9 9.7 %collective-permute-done.27 = f32[2,512,128]{2,1,0:T(8,128)S(1)} collective-permute-done((f32[2,512,128]{2,1,0:T(8,128)S(1)}, f32[2,512,128]{2,1,0:T(8,128)S(1)}, u32[]{:S(2)}, u32[]{:S(2)}) %collective-permute-start.27) | collective-permute-done | bytes 524320 | tf_op jit(solution)/shard_map/ppermute | solution.py:32
  (148 shorter events, 48.1 us)
Async XLA Ops:
  4.0 21.8 %collective-permute-start.6 = (bf16[192,4096]{1,0:T(8,128)(2,1)S(1)}, bf16[192,4096]{1,0:T(8,128)(2,1)}, u32[]{:S(2)}, u32[]{:S(2)}) collective-permute-start(bf16[192,4096]{1,0:T(8,128)(2,1)S(1)} %bitcast.126), channel_id=1, source_target_pairs={{0,1},{1,2},{2,3},{3,0},{4,5},{5,6},{6,7},{7,4},{8,9},{9,10},{10,1... | collective-permute-start | bytes 4718600 | tf_op jit(solution)/shard_map/ppermute | solution.py:32
  5.7 20.5 %collective-permute-start.2 = (bf16[192,4096]{1,0:T(8,128)(2,1)S(1)}, bf16[192,4096]{1,0:T(8,128)(2,1)}, u32[]{:S(2)}, u32[]{:S(2)}) collective-permute-start(bf16[192,4096]{1,0:T(8,128)(2,1)S(1)} %bitcast.118), channel_id=1, source_target_pairs={{0,64},{1,65},{2,66},{3,67},{4,68},{5,69},{6,70},{7,71},{8,72},{9,... | collective-permute-start | bytes 4718600 | tf_op jit(solution)/shard_map/ppermute | solution.py:32
  6.4 22.2 %collective-permute-start = (bf16[192,4096]{1,0:T(8,128)(2,1)S(1)}, bf16[192,4096]{1,0:T(8,128)(2,1)}, u32[]{:S(2)}, u32[]{:S(2)}) collective-permute-start(bf16[192,4096]{1,0:T(8,128)(2,1)S(1)} %bitcast.119), channel_id=1, source_target_pairs={{0,32},{1,33},{2,34},{3,35},{4,36},{5,37},{6,38},{7,39},{8,40},{9,... | collective-permute-start | bytes 4718600 | tf_op jit(solution)/shard_map/ppermute | solution.py:32
  7.2 22.3 %collective-permute-start.4 = (bf16[192,4096]{1,0:T(8,128)(2,1)S(1)}, bf16[192,4096]{1,0:T(8,128)(2,1)}, u32[]{:S(2)}, u32[]{:S(2)}) collective-permute-start(bf16[192,4096]{1,0:T(8,128)(2,1)S(1)} %bitcast.127), channel_id=1, source_target_pairs={{0,32},{1,33},{2,34},{3,35},{4,36},{5,37},{6,38},{7,39},{8,40},{9,... | collective-permute-start | bytes 4718600 | tf_op jit(solution)/shard_map/ppermute | solution.py:32
  26.2 14.0 %collective-permute-start.8 = (bf16[192,4096]{1,0:T(8,128)(2,1)}, bf16[192,4096]{1,0:T(8,128)(2,1)}, u32[]{:S(2)}, u32[]{:S(2)}) collective-permute-start(bf16[192,4096]{1,0:T(8,128)(2,1)} %collective-permute-done.2.refs_2_), channel_id=1, source_target_pairs={{0,32},{1,33},{2,34},{3,35},{4,36},{5,37},{6,38},{7,39},{8,40},{9,... | collective-permute-start | bytes 4718600 | tf_op jit(solution)/shard_map/ppermute | solution.py:32
  27.3 22.7 %collective-permute-start.3 = (bf16[192,4096]{1,0:T(8,128)(2,1)}, bf16[192,4096]{1,0:T(8,128)(2,1)}, u32[]{:S(2)}, u32[]{:S(2)}) collective-permute-start(bf16[192,4096]{1,0:T(8,128)(2,1)} %collective-permute-done.2.refs_2_), channel_id=1, source_target_pairs={{0,64},{1,65},{2,66},{3,67},{4,68},{5,69},{6,70},{7,71},{8,72},{9,... | collective-permute-start | bytes 4718600 | tf_op jit(solution)/shard_map/ppermute | solution.py:32
  28.6 36.3 %collective-permute-start.7 = (bf16[192,4096]{1,0:T(8,128)(2,1)}, bf16[192,4096]{1,0:T(8,128)(2,1)}, u32[]{:S(2)}, u32[]{:S(2)}) collective-permute-start(bf16[192,4096]{1,0:T(8,128)(2,1)} %collective-permute-done.6.refs_2_), channel_id=1, source_target_pairs={{0,1},{1,2},{2,3},{3,0},{4,5},{5,6},{6,7},{7,4},{8,9},{9,10},{10,1... | collective-permute-start | bytes 4718600 | tf_op jit(solution)/shard_map/ppermute | solution.py:32
  29.5 35.4 %collective-permute-start.1 = (bf16[192,4096]{1,0:T(8,128)(2,1)}, bf16[192,4096]{1,0:T(8,128)(2,1)}, u32[]{:S(2)}, u32[]{:S(2)}) collective-permute-start(bf16[192,4096]{1,0:T(8,128)(2,1)} %collective-permute-done.refs_1_), channel_id=1, source_target_pairs={{0,64},{1,65},{2,66},{3,67},{4,68},{5,69},{6,70},{7,71},{8,72},{9,... | collective-permute-start | bytes 4718600 | tf_op jit(solution)/shard_map/ppermute | solution.py:32
  29.8 37.6 %collective-permute-start.5 = (bf16[192,4096]{1,0:T(8,128)(2,1)}, bf16[192,4096]{1,0:T(8,128)(2,1)}, u32[]{:S(2)}, u32[]{:S(2)}) collective-permute-start(bf16[192,4096]{1,0:T(8,128)(2,1)} %collective-permute-done.4.refs_1_), channel_id=1, source_target_pairs={{0,1},{1,2},{2,3},{3,0},{4,5},{5,6},{6,7},{7,4},{8,9},{9,10},{10,1... | collective-permute-start | bytes 4718600 | tf_op jit(solution)/shard_map/ppermute | solution.py:32
  67.9 19.1 %collective-permute-start.12 = (bf16[192,4096]{1,0:T(8,128)(2,1)}, bf16[192,4096]{1,0:T(8,128)(2,1)S(1)}, u32[]{:S(2)}, u32[]{:S(2)}) collective-permute-start(bf16[192,4096]{1,0:T(8,128)(2,1)} %collective-permute-done.5.refs_0_), channel_id=1, source_target_pairs={{0,32},{1,33},{2,34},{3,35},{4,36},{5,37},{6,38},{7,39},{8,40},{9,... | collective-permute-start | bytes 4718600 | tf_op jit(solution)/shard_map/ppermute | solution.py:32
  67.9 19.1 %collective-permute-start.13 = (bf16[192,4096]{1,0:T(8,128)(2,1)}, bf16[192,4096]{1,0:T(8,128)(2,1)S(1)}, u32[]{:S(2)}, u32[]{:S(2)}) collective-permute-start(bf16[192,4096]{1,0:T(8,128)(2,1)} %collective-permute-done.7.refs_1_), channel_id=1, source_target_pairs={{0,32},{1,33},{2,34},{3,35},{4,36},{5,37},{6,38},{7,39},{8,40},{9,... | collective-permute-start | bytes 4718600 | tf_op jit(solution)/shard_map/ppermute | solution.py:32
  87.0 28.0 %collective-permute-start.14 = (f16[8,1040,128]{2,1,0:T(8,128)(2,1)}, f16[8,1040,128]{2,1,0:T(8,128)(2,1)}, u32[]{:S(2)}, u32[]{:S(2)}) collective-permute-start(f16[8,1040,128]{2,1,0:T(8,128)(2,1)} %bitcast.8), channel_id=1, source_target_pairs={{0,1},{1,2},{2,3},{3,0},{4,5},{5,6},{6,7},{7,4},{8,9},{9,10},{10,1... | collective-permute-start | bytes 6389768 | tf_op jit(solution)/shard_map/ppermute | solution.py:32
  100.5 26.7 %collective-permute-start.18 = (f16[8,1040,128]{2,1,0:T(8,128)(2,1)}, f16[8,1040,128]{2,1,0:T(8,128)(2,1)}, u32[]{:S(2)}, u32[]{:S(2)}) collective-permute-start(f16[8,1040,128]{2,1,0:T(8,128)(2,1)} %bitcast.21), channel_id=1, source_target_pairs={{0,64},{1,65},{2,66},{3,67},{4,68},{5,69},{6,70},{7,71},{8,72},{9,... | collective-permute-start | bytes 6389768 | tf_op jit(solution)/shard_map/ppermute | solution.py:32
  130.7 16.3 %collective-permute-start.16 = (f16[4,1040,128]{2,1,0:T(8,128)(2,1)S(1)}, f16[4,1040,128]{2,1,0:T(8,128)(2,1)S(1)}, u32[]{:S(2)}, u32[]{:S(2)}) collective-permute-start(f16[4,1040,128]{2,1,0:T(8,128)(2,1)S(1)} %get-tuple-element.98), channel_id=1, source_target_pairs={{0,1},{1,2},{2,3},{3,0},{4,5},{5,6},{6,7},{7,4},{8,9},{9,10},{10,1... | collective-permute-start | bytes 3194888 | tf_op jit(solution)/shard_map/ppermute | solution.py:32
  130.8 16.6 %collective-permute-start.20 = (f16[4,1040,128]{2,1,0:T(8,128)(2,1)S(1)}, f16[4,1040,128]{2,1,0:T(8,128)(2,1)S(1)}, u32[]{:S(2)}, u32[]{:S(2)}) collective-permute-start(f16[4,1040,128]{2,1,0:T(8,128)(2,1)S(1)} %get-tuple-element.99), channel_id=1, source_target_pairs={{0,64},{1,65},{2,66},{3,67},{4,68},{5,69},{6,70},{7,71},{8,72},{9,... | collective-permute-start | bytes 3194888 | tf_op jit(solution)/shard_map/ppermute | solution.py:32
  134.5 15.6 %collective-permute-start.15 = (f32[2,4,512,128]{3,2,1,0:T(8,128)S(1)}, f32[2,4,512,128]{3,2,1,0:T(8,128)S(1)}, u32[]{:S(2)}, u32[]{:S(2)}) collective-permute-start(f32[2,4,512,128]{3,2,1,0:T(8,128)S(1)} %pad_maximum_fusion), channel_id=1, source_target_pairs={{0,32},{1,33},{2,34},{3,35},{4,36},{5,37},{6,38},{7,39},{8,40},{9,... | collective-permute-start | bytes 6291464 | tf_op jit(solution)/shard_map/ppermute | solution.py:32
  136.3 16.4 %collective-permute-start.19 = (f32[2,4,512,128]{3,2,1,0:T(8,128)S(1)}, f32[2,4,512,128]{3,2,1,0:T(8,128)S(1)}, u32[]{:S(2)}, u32[]{:S(2)}) collective-permute-start(f32[2,4,512,128]{3,2,1,0:T(8,128)S(1)} %pad_maximum_fusion.1), channel_id=1, source_target_pairs={{0,32},{1,33},{2,34},{3,35},{4,36},{5,37},{6,38},{7,39},{8,40},{9,... | collective-permute-start | bytes 6291464 | tf_op jit(solution)/shard_map/ppermute | solution.py:32
  151.4 12.1 %collective-permute-start.22 = (f32[1,512,128]{2,1,0:T(8,128)}, f32[1,512,128]{2,1,0:T(8,128)}, u32[]{:S(2)}, u32[]{:S(2)}) collective-permute-start(f32[1,512,128]{2,1,0:T(8,128)} %get-tuple-element.91), channel_id=1, source_target_pairs={{0,4},{1,5},{2,6},{3,7},{4,8},{5,9},{6,10},{7,11},{8,12},{9,13},{1... | collective-permute-start | bytes 786440 | tf_op jit(solution)/shard_map/ppermute | solution.py:32
  168.1 15.4 %collective-permute-start.23 = (f32[2,512,128]{2,1,0:T(8,128)}, f32[2,512,128]{2,1,0:T(8,128)}, u32[]{:S(2)}, u32[]{:S(2)}) collective-permute-start(f32[2,512,128]{2,1,0:T(8,128)} %pad_maximum_fusion.5), channel_id=1, source_target_pairs={{0,4},{1,5},{2,6},{3,7},{4,8},{5,9},{6,10},{7,11},{8,12},{9,13},{1... | collective-permute-start | bytes 1572872 | tf_op jit(solution)/shard_map/ppermute | solution.py:32
  169.0 14.7 %collective-permute-start.25 = (f32[2,512,128]{2,1,0:T(8,128)}, f32[2,512,128]{2,1,0:T(8,128)}, u32[]{:S(2)}, u32[]{:S(2)}) collective-permute-start(f32[2,512,128]{2,1,0:T(8,128)} %pad_maximum_fusion.6), channel_id=1, source_target_pairs={{0,28},{1,29},{2,30},{3,31},{4,0},{5,1},{6,2},{7,3},{8,4},{9,5},{1... | collective-permute-start | bytes 1572872 | tf_op jit(solution)/shard_map/ppermute | solution.py:32
  185.0 14.4 %collective-permute-start.26 = (f32[2,512,128]{2,1,0:T(8,128)S(1)}, f32[2,512,128]{2,1,0:T(8,128)S(1)}, u32[]{:S(2)}, u32[]{:S(2)}) collective-permute-start(f32[2,512,128]{2,1,0:T(8,128)S(1)} %get-tuple-element.80), channel_id=1, source_target_pairs={{0,4},{1,5},{2,6},{3,7},{4,8},{5,9},{6,10},{7,11},{8,12},{9,13},{1... | collective-permute-start | bytes 1572872 | tf_op jit(solution)/shard_map/ppermute | solution.py:32
  187.5 12.0 %collective-permute-start.28 = (f32[2,512,128]{2,1,0:T(8,128)S(1)}, f32[2,512,128]{2,1,0:T(8,128)S(1)}, u32[]{:S(2)}, u32[]{:S(2)}) collective-permute-start(f32[2,512,128]{2,1,0:T(8,128)S(1)} %get-tuple-element.81), channel_id=1, source_target_pairs={{0,28},{1,29},{2,30},{3,31},{4,0},{5,1},{6,2},{7,3},{8,4},{9,5},{1... | collective-permute-start | bytes 1572872 | tf_op jit(solution)/shard_map/ppermute | solution.py:32
  199.6 13.0 %collective-permute-start.27 = (f32[2,512,128]{2,1,0:T(8,128)S(1)}, f32[2,512,128]{2,1,0:T(8,128)S(1)}, u32[]{:S(2)}, u32[]{:S(2)}) collective-permute-start(f32[2,512,128]{2,1,0:T(8,128)S(1)} %get-tuple-element.78), channel_id=1, source_target_pairs={{0,4},{1,5},{2,6},{3,7},{4,8},{5,9},{6,10},{7,11},{8,12},{9,13},{1... | collective-permute-start | bytes 1572872 | tf_op jit(solution)/shard_map/ppermute | solution.py:32
  200.8 11.8 %collective-permute-start.29 = (f32[2,512,128]{2,1,0:T(8,128)S(1)}, f32[2,512,128]{2,1,0:T(8,128)S(1)}, u32[]{:S(2)}, u32[]{:S(2)}) collective-permute-start(f32[2,512,128]{2,1,0:T(8,128)S(1)} %get-tuple-element.79), channel_id=1, source_target_pairs={{0,28},{1,29},{2,30},{3,31},{4,0},{5,1},{6,2},{7,3},{8,4},{9,5},{1... | collective-permute-start | bytes 1572872 | tf_op jit(solution)/shard_map/ppermute | solution.py:32
  (29 other events, 192.0 us)
